TPU v7x, 256 devices: a whole 4x4x8 slice. The times are simulated.
256 devices in a mesh: seq: 64 (over y, z_hi, x), tp: 4 (over z_lo, core).
Axes of the slice: x: 4, y: 4, z: 8 (z_hi: 4, z_lo: 2; z = z_hi * 2 + z_lo), core: 2. Of those that a mesh axis runs over, the one named last changes fastest.
Arguments:
- tokens: bfloat16 [32256, 4096], P('seq'), may hold values from -6 to 6
- norm_gain: float32 [4096], replicated, may hold values from 0.5 to 1.5
- gate_weight: bfloat16 [4096, 7168], P('seq', 'tp'), may hold values from -0.09375 to 0.09375
- up_weight: bfloat16 [4096, 7168], P('seq', 'tp'), may hold values from -0.09375 to 0.09375
Outputs:
- saved_hidden: bfloat16 [32256, 7168], P('seq', 'tp')
- token_scales: float32 [32256], P('seq')
All inputs are finite; a program needn't handle non-finite values. Where the computation divides by a largest or mean magnitude, that divisor is 1e-20 or more.
Results may differ from a plain program's by a relative error of at most 0.0061.
Values may be sent and summed in bfloat16 or wider, within the bound.
A program may use at most 128 MiB of HBM per device.

v0:
```python
import jax
import jax.numpy as jnp
from jax import lax
from jax.sharding import PartitionSpec as P


def norm_rows(block, norm_gain):
    values = block.astype(jnp.float32)
    mean_square = jnp.mean(values * values, axis=1, keepdims=True)
    return (values * lax.rsqrt(mean_square + 1e-05) * norm_gain[None, :]).astype(jnp.bfloat16)


def add_rows(normed, piece):
    return jnp.dot(normed, piece, preferred_element_type=jnp.float32)


def shards(tokens, norm_gain, gate_weight, up_weight):
    normed = norm_rows(tokens, norm_gain)

    def add_single(piece):
        return add_rows(normed, piece)

    gate = add_single(lax.all_gather(gate_weight, "seq", axis=0, tiled=True))
    up = add_single(lax.all_gather(up_weight, "seq", axis=0, tiled=True))
    hidden = jax.nn.silu(gate) * up
    local_peak = jnp.max(jnp.abs(hidden), axis=1)
    scales = lax.pmax(local_peak, "tp") + 1e-06
    saved = (hidden / scales[:, None]).astype(jnp.bfloat16)
    return (saved, scales)


def solution(mesh):
    in_specs = (P("seq", None), P(), P("seq", "tp"), P("seq", "tp"))
    out_specs = (P("seq", "tp"), P("seq"))
    return jax.shard_map(shards, mesh=mesh, in_specs=in_specs, out_specs=out_specs, check_vma=False)
```

profile of v0, /device:TPU:4, one launch (start us, length us, event | category | flops | bytes accessed | tf_op | source)
XLA Modules:
  0.0 360.7 jit_solution(13655028735498425475)
XLA Ops:
  7.2 0.0 copy-start.1
  7.2 0.0 all-gather.3.cloned.1.call-start
  7.2 0.7 all-gather.3.cloned.1.call-update
  7.9 0.0 all-gather.5.cloned.1.call-start
  8.0 0.7 all-gather.5.cloned.1.call-update
  8.7 3.1 fusion
  11.7 143.4 %all-gather.3.cloned.1.call-done = bf16[4096,1792]{1,0:T(8,128)(2,1)} async-done(((bf16[64,1792]{1,0:T(8,128)(2,1)}), bf16[4096,1792]{1,0:T(8,128)(2,1)}) %all-gather.3.cloned.1.call-update) | async-done | bytes 14680080 | tf_op jit(solution)/shard_map/all_gather | solution.py:23
  155.1 0.0 copy-done.1
  155.1 14.5 %fusion.4 = f32[504,1792]{1,0:T(8,128)} fusion(bf16[4096,1792]{1,0:T(8,128)(2,1)} %all-gather.3.cloned.1.call-done, bf16[504,4096]{1,0:T(8,128)(2,1)} %param.4, f32[4096]{0:T(1024)S(1)} %copy-done.1, f32[504]{0:T(512)S(1)} %add_rsqrt_fusion), kind=kOutput, calls=%fused_computation.8 | convolution fusion | flops 7407009792 | bytes 22439904 | tf_op jit(solution)/shard_map/dot_general | solution.py:14
  169.6 142.6 %all-gather.5.cloned.1.call-done = bf16[4096,1792]{1,0:T(8,128)(2,1)} async-done(((bf16[64,1792]{1,0:T(8,128)(2,1)}), bf16[4096,1792]{1,0:T(8,128)(2,1)}) %all-gather.5.cloned.1.call-update) | async-done | bytes 14680080 | tf_op jit(solution)/shard_map/all_gather | solution.py:24
  312.3 16.1 %abs_reduce_fusion = (f32[504]{0:T(512)S(1)}, f32[504,1792]{1,0:T(8,128)}) fusion(bf16[4096,1792]{1,0:T(8,128)(2,1)} %all-gather.5.cloned.1.call-done, bf16[504,4096]{1,0:T(8,128)(2,1)} %param.4, f32[4096]{0:T(1024)S(1)} %copy-done.1, f32[504]{0:T(512)S(1)} %add_rsqrt_fusion, f32[504,1792]{1,0:T(8,128)} %fusion.4), kind=kOutput, calls=%fused_computation.6 | convolution fusion | flops 7413331456 | bytes 26054592 | tf_op jit(solution)/shard_map/dot_general | solution.py:14
  328.4 21.8 %pmax.7 = f32[504]{0:T(512)S(1)} all-reduce(f32[504]{0:T(512)S(1)} %get-tuple-element.2), channel_id=1, replica_groups=mesh['seq'=64,'tp'=4] {'tp'}, use_global_device_ids=true, to_apply=%region_2.3 | all-reduce | flops 504 | bytes 4032 | tf_op jit(solution)/shard_map/pmax | solution.py:27
  350.2 0.0 copy-start
  350.2 3.6 %divide_convert_fusion = bf16[504,1792]{1,0:T(8,128)(2,1)} fusion(f32[504,1792]{1,0:T(8,128)} %get-tuple-element.3, f32[504]{0:T(512)S(1)} %broadcast_add_fusion), kind=kLoop, calls=%fused_computation.5 | loop fusion | flops 1806336 | bytes 5421024 | tf_op jit(solution)/shard_map/convert_element_type | solution.py:28
  353.8 0.0 copy-done
  (2 shorter events, 0.0 us)
Async XLA Ops:
  7.2 147.9 %copy-start.1 = (f32[4096]{0:T(1024)S(1)}, f32[4096]{0:T(1024)}, u32[]{:S(2)}) copy-start(f32[4096]{0:T(1024)} %param.5) | copy-start | bytes 49156
  7.2 147.9 %all-gather.3.cloned.1.call-start = ((), (), s32[]{:S(2)}) async-start(), calls=%async_computation | async-start | bytes 14909440 | tf_op jit(solution)/shard_map/all_gather | solution.py:23
  7.9 304.4 %all-gather.5.cloned.1.call-start = ((), (), s32[]{:S(2)}) async-start(), calls=%async_computation.1 | async-start | bytes 14909440 | tf_op jit(solution)/shard_map/all_gather | solution.py:24
  350.2 3.6 %copy-start = (f32[504]{0:T(512)}, f32[504]{0:T(512)S(1)}, u32[]{:S(2)}) copy-start(f32[504]{0:T(512)S(1)} %broadcast_add_fusion) | copy-start | bytes 6052
Sparse Core Ops, SparseCore 0:
  11.3 143.7 all-gather.2
  158.4 153.8 all-gather.4
where the time goes:
time: 361 us
  waiting for transfers between devices  287 us (80%)
  matrix products  30.6 us (8%)
  blocking collectives  21.8 us (6%)
  between operations  14 us (4%)
  other arithmetic  6.69 us (2%)
    all_gather x1, waiting for transfers between devices, shards(): gate = add_single(lax.all_gather(gate_weight, 'seq', axis=0, tiled=True))  143 us
    all_gather x1, waiting for transfers between devices, shards(): up = add_single(lax.all_gather(up_weight, 'seq', axis=0, tiled=True))  143 us
    dot_general x2, matrix products, add_rows(): return jnp.dot(normed, piece, preferred_element_type=jnp.float32)  30.6 us
    pmax x1, blocking collectives, shards(): scales = lax.pmax(local_peak, 'tp') + 1e-06  21.8 us
  transfers between devices with their start and end apart: 2, of which 2 were waited for; matrix products, arithmetic and copies ran while one was open for 5% of the time, Pallas kernels for 0%

commit v1 on v0

--- a/solution.py
+++ b/solution.py
@@ -21,7 +21,11 @@
         return add_rows(normed, piece)
 
     gate = add_single(lax.all_gather(gate_weight, "seq", axis=0, tiled=True))
-    up = add_single(lax.all_gather(up_weight, "seq", axis=0, tiled=True))
+    up = add_single(
+        jnp.concatenate(
+            lax.all_to_all(jnp.stack([up_weight] * lax.axis_size("seq")), "seq", 0, 0), axis=0
+        )
+    )
     hidden = jax.nn.silu(gate) * up
     local_peak = jnp.max(jnp.abs(hidden), axis=1)
     scales = lax.pmax(local_peak, "tp") + 1e-06

time: 361 us -> 505 us (1.40)
  waiting for transfers between devices: 287 us -> 410 us
  starting transfers between devices: 0.08 us -> 14.8 us
  local copies, waits for them, and re-layouts: 0.01 us -> 7.95 us
    all_gather x1, waiting for transfers between devices: 143 us -> 391 us  [shards(): gate = add_single(lax.all_gather(gate_weight, 'seq', axis=0, tiled=True))]
    all_gather x1 -> x0, waiting for transfers between devices: 143 us -> none  [shards(): up = add_single(lax.all_gather(up_weight, 'seq', axis=0, tiled=True))]
    all_to_all x0 -> x1, waiting for transfers between devices: none -> 18.1 us  [shards(): lax.all_to_all(jnp.stack([up_weight] * lax.axis_size('seq')), 'seq', 0, 0)]
    all_to_all x0 -> x1, starting transfers between devices: none -> 14.8 us  [shards(): lax.all_to_all(jnp.stack([up_weight] * lax.axis_size('seq')), 'seq', 0, 0)]
    another operation x0 -> x1, local copies, waits for them, and re-layouts: none -> 7.94 us  [shards(): jnp.stack([up_weight] * lax.axis_size('seq'))]
where the time goes in v1:
time: 505 us
  waiting for transfers between devices  410 us (81%)
  matrix products  30.7 us (6%)
  blocking collectives  20.2 us (4%)
  starting transfers between devices  14.8 us (3%)
  between operations  14 us (3%)
  local copies, waits for them, and re-layouts  7.95 us (2%)
  other arithmetic  6.7 us (1%)
    all_gather x1, waiting for transfers between devices, shards(): gate = add_single(lax.all_gather(gate_weight, 'seq', axis=0, tiled=True))  391 us
    dot_general x2, matrix products, add_rows(): return jnp.dot(normed, piece, preferred_element_type=jnp.float32)  30.7 us
    pmax x1, blocking collectives, shards(): scales = lax.pmax(local_peak, 'tp') + 1e-06  20.2 us
    all_to_all x1, waiting for transfers between devices, shards(): lax.all_to_all(jnp.stack([up_weight] * lax.axis_size('seq')), 'seq', 0, 0)  18.1 us
    all_to_all x1, starting transfers between devices, shards(): lax.all_to_all(jnp.stack([up_weight] * lax.axis_size('seq')), 'seq', 0, 0)  14.8 us
  transfers between devices with their start and end apart: 2, of which 2 were waited for; matrix products, arithmetic and copies ran while one was open for 5% of the time, Pallas kernels for 0%

profile of v1, /device:TPU:4, one launch (start us, length us, event | category | flops | bytes accessed | tf_op | source)
XLA Modules:
  0.0 504.7 jit_solution(9573004872556881066)
XLA Ops:
  7.2 0.0 all-gather.2.cloned.1.call-start
  7.2 0.7 all-gather.2.cloned.1.call-update
  7.9 7.9 %stack.2 = bf16[64,64,1792]{2,1,0:T(8,128)(2,1)} broadcast(bf16[64,1792]{1,0:T(8,128)(2,1)} %param.7), dimensions={1,2} | broadcast | bytes 14909440 | tf_op jit(solution)/shard_map/stack | solution.py:26
  15.8 14.8 %all-to-all-start = ((bf16[64,64,1792]{2,1,0:T(8,128)(2,1)}), bf16[64,64,1792]{2,1,0:T(8,128)(2,1)}, u32[]{:S(2)}, u32[]{:S(2)}) async-start(bf16[64,64,1792]{2,1,0:T(8,128)(2,1)} %stack.2), calls=%async_computation | async-start | bytes 29360128 | tf_op jit(solution)/shard_map/all_to_all | solution.py:26
  30.6 0.0 copy-start.1
  30.6 3.1 fusion
  33.7 391.4 %all-gather.2.cloned.1.call-done = bf16[4096,1792]{1,0:T(8,128)(2,1)} async-done(((bf16[64,1792]{1,0:T(8,128)(2,1)}), bf16[4096,1792]{1,0:T(8,128)(2,1)}) %all-gather.2.cloned.1.call-update) | async-done | bytes 14680080 | tf_op jit(solution)/shard_map/all_gather | solution.py:23
  425.1 0.0 copy-done.1
  425.1 14.6 %fusion.4 = f32[504,1792]{1,0:T(8,128)} fusion(bf16[4096,1792]{1,0:T(8,128)(2,1)} %all-gather.2.cloned.1.call-done, bf16[504,4096]{1,0:T(8,128)(2,1)} %param.4, f32[4096]{0:T(1024)S(1)} %copy-done.1, f32[504]{0:T(512)S(1)} %add_rsqrt_fusion), kind=kOutput, calls=%fused_computation.8 | convolution fusion | flops 7407009792 | bytes 22439904 | tf_op jit(solution)/shard_map/dot_general | solution.py:14
  439.7 18.1 %all-to-all-done = bf16[64,64,1792]{2,1,0:T(8,128)(2,1)} async-done(((bf16[64,64,1792]{2,1,0:T(8,128)(2,1)}), bf16[64,64,1792]{2,1,0:T(8,128)(2,1)}, u32[]{:S(2)}, u32[]{:S(2)}) %all-to-all-start) | async-done | bytes 14680096 | tf_op jit(solution)/shard_map/all_to_all | solution.py:26
  457.8 16.1 %abs_reduce_fusion = (f32[504]{0:T(512)S(1)}, f32[504,1792]{1,0:T(8,128)}) fusion(bf16[4096,1792]{1,0:T(8,128)(2,1)} %bitcast, bf16[504,4096]{1,0:T(8,128)(2,1)} %param.4, f32[4096]{0:T(1024)S(1)} %copy-done.1, f32[504]{0:T(512)S(1)} %add_rsqrt_fusion, f32[504,1792]{1,0:T(8,128)} %fusion.4), kind=kOutput, calls=%fused_computation.6 | convolution fusion | flops 7413331456 | bytes 26054592 | tf_op jit(solution)/shard_map/dot_general | solution.py:14
  473.9 20.2 %pmax.7 = f32[504]{0:T(512)S(1)} all-reduce(f32[504]{0:T(512)S(1)} %get-tuple-element.2), channel_id=1, replica_groups=mesh['seq'=64,'tp'=4] {'tp'}, use_global_device_ids=true, to_apply=%region_2.3 | all-reduce | flops 504 | bytes 4032 | tf_op jit(solution)/shard_map/pmax | solution.py:31
  494.2 0.0 copy-start
  494.2 3.6 divide_convert_fusion
  497.8 0.0 copy-done
  (2 shorter events, 0.0 us)
Async XLA Ops:
  7.2 417.9 %all-gather.2.cloned.1.call-start = ((), (), s32[]{:S(2)}) async-start(), calls=%async_computation.1 | async-start | bytes 14909440 | tf_op jit(solution)/shard_map/all_gather | solution.py:23
  15.8 442.0 %all-to-all-start = ((bf16[64,64,1792]{2,1,0:T(8,128)(2,1)}), bf16[64,64,1792]{2,1,0:T(8,128)(2,1)}, u32[]{:S(2)}, u32[]{:S(2)}) async-start(bf16[64,64,1792]{2,1,0:T(8,128)(2,1)} %stack.2), calls=%async_computation | async-start | bytes 29360128 | tf_op jit(solution)/shard_map/all_to_all | solution.py:26
  30.6 394.5 %copy-start.1 = (f32[4096]{0:T(1024)S(1)}, f32[4096]{0:T(1024)}, u32[]{:S(2)}) copy-start(f32[4096]{0:T(1024)} %param.5) | copy-start | bytes 49156
  494.2 3.6 copy-start
Sparse Core Ops, SparseCore 0:
  11.3 413.7 all-gather.1
